TPU v7x, 32 devices: a whole 2x2x4 slice. The times are simulated.
32 devices in a mesh: groups: 2 (over y), edge: 4 (over z), replica: 2 (over x), probe: 2 (over core).
Axes of the slice: x: 2, y: 2, z: 4, core: 2. Of those that a mesh axis runs over, the one named last changes fastest.
Arguments:
- edge_feats: bfloat16 [4, 6144, 256], P(('groups', 'replica'), 'edge'), parts along dimension 0, may hold values from -6 to 6
- edge_vecs: float32 [4, 3, 6144], P(('groups', 'replica'), None, 'edge'), parts along dimension 0, may hold values from -2 to 2
- senders: int32 [4, 6144], P(('groups', 'replica'), 'edge'), parts along dimension 0, may hold values from 0 to 1023
- receivers: int32 [4, 6144], P(('groups', 'replica'), 'edge'), parts along dimension 0, may hold values from 0 to 1023
- tiles: bfloat16 [4, 128, 128, 128], P(('groups', 'replica'), 'edge'), parts along dimension 0, may hold values from -0.5 to 0.5
- tile_rows: int32 [4, 128], P(('groups', 'replica'), 'edge'), parts along dimension 0, may hold values from 0 to 23
- tile_cols: int32 [4, 128], P(('groups', 'replica'), 'edge'), parts along dimension 0, may hold values from 0 to 23
- tile_count: int32 [4, 4], P(('groups', 'replica'), 'edge'), parts along dimension 0, may hold values from 1 to 32, as said below
- probes: int32 [3072, 128], P(None, 'probe'), may hold values from -1 to 1, as said below
- w_in: bfloat16 [256, 256], replicated, may hold values from -0.375 to 0.375
- w_msg: bfloat16 [256, 128], replicated, may hold values from -0.375 to 0.375
- w_stiff: bfloat16 [256], replicated, may hold values from -0.375 to 0.375
- w_env: float32 [128], replicated, may hold values from -0.1875 to 0.1875
Outputs:
- residual: float32 [4, 3072, 128], P(('groups', 'replica'), None, 'probe'), parts along dimension 0
- mse: float32 [4], P(('groups', 'replica')), parts along dimension 0
- grad_in: float32 [512, 256], P('groups'), parts along dimension 0
- grad_msg: float32 [512, 128], P('groups'), parts along dimension 0
- grad_stiff: float32 [512], P('groups'), parts along dimension 0
- grad_env: float32 [256], P('groups'), parts along dimension 0
There are 2 independent parts, one for each index of `groups`. A program takes and returns all parts, laid end to end along the dimension named above; an argument that names none is the same for every part. Nothing has to cross between parts.
Inputs may be any that keep to these rules, and one draw needn't show every extreme that they name: `probes`: entries are -1 or 1. `tile_count`: in every structure some owner has all 32 slots live.
All inputs are finite; a program needn't handle non-finite values.
Results may differ from a plain program's by a relative error of at most 0.0018.
Values sent between devices are 32-bit elements; how exact they have to be, the bound alone decides.
A program may use at most 64 MiB of HBM per device.

v0:
```python
import jax
import jax.numpy as jnp
from jax import lax
from jax.sharding import PartitionSpec as P

TILE = 128
PROBES = 128


HI = lax.Precision.HIGHEST


def body(
    edge_feats,
    edge_vecs,
    senders,
    receivers,
    tiles,
    tile_rows,
    tile_cols,
    tile_count,
    probes,
    w_in,
    w_msg,
    w_stiff,
    w_env,
):
    feats = edge_feats[0]
    vecs = edge_vecs[0]
    send = senders[0]
    recv = receivers[0]
    tls = tiles[0]
    rows = tile_rows[0]
    cols = tile_cols[0]
    count = tile_count[0, 0]
    share = probes.shape[1]
    n_slots = tls.shape[0]
    n_blocks = probes.shape[0] // TILE
    n_atoms = probes.shape[0] // 3
    contract = (((0,), (0,)), ((), ()))
    live = (jnp.arange(n_slots, dtype=jnp.int32) < count).astype(jnp.float32)
    blocks = probes.astype(jnp.bfloat16).reshape(n_blocks, TILE, share)[cols]
    prod = jnp.einsum("tij,tjp->tip", tls, blocks, preferred_element_type=jnp.float32)
    rowhot = (rows[:, None] == jnp.arange(n_blocks, dtype=jnp.int32)[None, :]).astype(
        jnp.float32
    ) * live[:, None]
    ref_part = jnp.einsum("tb,tip->bip", rowhot, prod, precision=HI).reshape(3 * n_atoms, share)
    atom_ids = jnp.arange(n_atoms, dtype=jnp.int32)[None, :]
    pre = jnp.dot(feats, w_in, preferred_element_type=jnp.float32)
    latent = jax.nn.silu(pre).astype(jnp.bfloat16)
    message = jnp.dot(latent, w_msg, preferred_element_type=jnp.float32).astype(jnp.bfloat16)
    recv_hot = (recv[:, None] == atom_ids).astype(jnp.bfloat16)
    env_part = lax.dot_general(recv_hot, message, contract, preferred_element_type=jnp.float32)
    env = lax.psum(env_part, "edge")
    env_recv = jnp.take(env, recv, axis=0)
    zeta_own = jnp.dot(latent, w_stiff, preferred_element_type=jnp.float32) + jnp.dot(
        env_recv, w_env, precision=HI
    )
    stiff = jax.nn.softplus(zeta_own)
    signed_hot = (send[:, None] == atom_ids).astype(jnp.bfloat16) - (
        recv[:, None] == atom_ids
    ).astype(jnp.bfloat16)
    pflat = probes.reshape(n_atoms, 3 * share)
    delta = (
        (jnp.take(pflat, send, axis=0) - jnp.take(pflat, recv, axis=0))
        .astype(jnp.float32)
        .reshape(-1, 3, share)
    )
    proj = jnp.einsum("ce,ecp->ep", vecs, delta, precision=HI)
    contrib = (stiff[:, None, None] * vecs.T[:, :, None] * proj[:, None, :]).astype(jnp.bfloat16)
    model_part = lax.dot_general(
        signed_hot, contrib.reshape(-1, 3 * share), contract, preferred_element_type=jnp.float32
    )
    model_part = model_part.reshape(3 * n_atoms, share)
    residual = lax.psum(model_part - ref_part, "edge")
    rflat = residual.reshape(n_atoms, 3 * share)
    rdiff = (jnp.take(rflat, send, axis=0) - jnp.take(rflat, recv, axis=0)).reshape(-1, 3, share)
    rproj = jnp.einsum("ce,ecp->ep", vecs, rdiff, precision=HI)
    dstiff_part = 2.0 / PROBES * jnp.sum(proj * rproj, axis=1)
    square_part = jnp.sum(residual * residual)
    dstiff, square_sum = lax.psum((dstiff_part, square_part), "probe")
    mse = (square_sum / (3 * n_atoms * PROBES)).reshape(1)
    dzeta = dstiff * jax.nn.sigmoid(zeta_own)
    weight = lax.psum(jax.ops.segment_sum(dzeta, recv, n_atoms), "edge")
    dzeta_b = dzeta.astype(jnp.bfloat16)
    dmsg = (jnp.take(weight, recv, axis=0)[:, None] * w_env[None, :]).astype(jnp.bfloat16)
    dlat = dzeta[:, None] * w_stiff.astype(jnp.float32)[None, :] + lax.dot_general(
        dmsg, w_msg, (((1,), (1,)), ((), ())), preferred_element_type=jnp.float32
    )
    sig = jax.nn.sigmoid(pre)
    dpre = (dlat * sig * (1.0 + pre * (1.0 - sig))).astype(jnp.bfloat16)
    g_in = lax.dot_general(feats, dpre, contract, preferred_element_type=jnp.float32)
    g_msg = lax.dot_general(latent, dmsg, contract, preferred_element_type=jnp.float32)
    g_stiff = jnp.dot(dzeta_b, latent, preferred_element_type=jnp.float32)
    g_env = jnp.dot(dzeta, env_recv, precision=HI)
    g_in, g_msg, g_stiff, g_env = lax.psum((g_in, g_msg, g_stiff, g_env), ("edge", "replica"))
    return (residual.reshape(1, 3 * n_atoms, share), mse, g_in, g_msg, g_stiff, g_env)


def solution(mesh):
    return jax.shard_map(
        body,
        mesh=mesh,
        in_specs=(
            P(("groups", "replica"), "edge", None),
            P(("groups", "replica"), None, "edge"),
            P(("groups", "replica"), "edge"),
            P(("groups", "replica"), "edge"),
            P(("groups", "replica"), "edge", None, None),
            P(("groups", "replica"), "edge"),
            P(("groups", "replica"), "edge"),
            P(("groups", "replica"), "edge"),
            P(None, "probe"),
            P(),
            P(),
            P(),
            P(),
        ),
        out_specs=(
            P(("groups", "replica"), None, "probe"),
            P(("groups", "replica")),
            P("groups", None),
            P("groups", None),
            P("groups"),
            P("groups"),
        ),
        check_vma=False,
    )
```

profile of v0, /device:TPU:0, one launch (start us, length us, event | category | flops | bytes accessed | tf_op | source)
XLA Modules:
  0.0 273.5 jit_solution(12682948379534146705)
XLA Ops:
  8.0 2.8 %multiply_convert_fusion = (bf16[1536,256]{1,0:T(8,128)(2,1)S(1)}, f32[1536,256]{1,0:T(8,128)}) fusion(bf16[256,256]{1,0:T(8,128)(2,1)} %param.26, bf16[1,1536,256]{2,1,0:T(8,128)(2,1)} %param.17), kind=kOutput, calls=%fused_computation.28 | convolution fusion | flops 203292672 | bytes 3276800 | tf_op jit(solution)/shard_map/dot_general | solution.py:49
  10.9 2.9 %fusion = f32[1024,128]{1,0:T(8,128)} fusion(s32[1536]{0:T(1024)S(1)} %reduce.3, bf16[1536,256]{1,0:T(8,128)(2,1)S(1)} %get-tuple-element.34, bf16[256,128]{1,0:T(8,128)(2,1)S(1)} %copy-done.10), kind=kOutput, calls=%fused_computation.9 | convolution fusion | flops 505085952 | bytes 1382400 | tf_op jit(solution)/shard_map/dot_general | solution.py:53
  17.8 4.7 %gather_fusion.4 = s32[1536,192]{1,0:T(8,128)} fusion(s32[1024,192]{1,0:T(8,128)S(1)} %reshape.146, s32[2048]{0:T(1024)S(1)} %pad_clamp_fusion), kind=kCustom, calls=%fused_computation.2.clone | custom fusion | bytes 2365440 | tf_op jit(solution)/shard_map/jit(_take)/gather | solution.py:65
  22.5 4.7 %gather_fusion.3 = s32[1536,192]{1,0:T(8,128)} fusion(s32[1024,192]{1,0:T(8,128)S(1)} %reshape.146, s32[2048]{0:T(1024)S(1)} %pad_clamp_fusion.1), kind=kCustom, calls=%fused_computation.clone | custom fusion | bytes 2365440 | tf_op jit(solution)/shard_map/jit(_take)/gather | solution.py:65
  27.2 2.4 fusion.13
  33.3 2.2 fusion.17
  37.6 2.2 multiply_reduce_fusion.2
  39.7 15.2 %all-reduce.7.cloned.1.call-done = f32[1024,128]{1,0:T(8,128)} async-done(((f32[1024,128]{1,0:T(8,128)}), f32[1024,128]{1,0:T(8,128)}) %all-reduce.7.cloned.1.call-update) | async-done | bytes 524304 | tf_op jit(solution)/shard_map/psum | solution.py:54
  54.9 3.6 %gather_fusion = f32[1536,128]{1,0:T(8,128)S(1)} fusion(f32[1024,128]{1,0:T(8,128)} %all-reduce.7.cloned.1.call-done, s32[2048]{0:T(1024)S(1)} %pad_clamp_fusion.2), kind=kCustom, calls=%fused_computation.4 | custom fusion | bytes 1579008 | tf_op jit(solution)/shard_map/jit(_take)/gather | solution.py:55
  60.6 2.8 %fusion.4 = f32[1024,192]{1,0:T(8,128)} fusion(bf16[1536,192]{0,1:T(8,128)(2,1)S(1)} %bitcast.73, s32[1536]{0:T(1024)S(1)} %reduce.3, s32[1536]{0:T(1024)S(1)} %reduce.2), kind=kOutput, calls=%fused_computation.14 | convolution fusion | flops 616562688 | bytes 1388544 | tf_op jit(solution)/shard_map/dot_general | solution.py:71
  63.4 2.6 reshape.148
  66.0 2.7 bitcast_subtract_fusion
  69.0 69.0 %all-reduce.9.cloned.1.call-done = f32[3072,64]{1,0:T(8,128)} async-done(((f32[3072,64]{1,0:T(8,128)}), f32[3072,64]{1,0:T(8,128)}) %all-reduce.9.cloned.1.call-update) | async-done | bytes 786448 | tf_op jit(solution)/shard_map/psum | solution.py:75
  139.9 4.7 %gather_fusion.6 = f32[1536,192]{1,0:T(8,128)} fusion(f32[1024,192]{1,0:T(8,128)S(1)} %reshape.153, s32[2048]{0:T(1024)S(1)} %pad_clamp_fusion), kind=kCustom, calls=%fused_computation.3.clone | custom fusion | bytes 2365440 | tf_op jit(solution)/shard_map/jit(_take)/gather | solution.py:77
  144.6 4.7 %gather_fusion.5 = f32[1536,192]{1,0:T(8,128)} fusion(f32[1024,192]{1,0:T(8,128)S(1)} %reshape.153, s32[2048]{0:T(1024)S(1)} %pad_clamp_fusion.1), kind=kCustom, calls=%fused_computation.1.clone | custom fusion | bytes 2365440 | tf_op jit(solution)/shard_map/jit(_take)/gather | solution.py:77
  149.3 2.4 select_subtract_fusion
  156.7 3.1 %all-reduce.2 = (f32[]{:T(128)}, f32[1536]{0:T(1024)S(1)}) all-reduce(f32[]{:T(128)} %multiply_reduce_fusion, f32[1536]{0:T(1024)S(1)} %broadcast_multiply_fusion), channel_id=1, replica_groups=mesh['groups'=2,'edge'=4,'replica'=2,'probe'=2] {'probe'}, use_global_device_ids=true, to_apply=%region_3.5 | all-reduce | flops 1537 | bytes 12296 | tf_op jit(solution)/shard_map/psum | solution.py:81
  159.9 11.1 %scatter_custom_fusion = f32[1024]{0:T(1024)S(1)} fusion(s32[1536]{0:T(1024)S(1)} %reduce.3, f32[1536]{0:T(1024)S(1)} %get-tuple-element.33, f32[]{:T(128)} %constant.49.clone.1), kind=kCustom, calls=%fused_computation.88 | custom fusion | flops 1536 | bytes 4100 | tf_op jit(solution)/shard_map/scatter-add | solution.py:84
  171.0 9.8 %psum.67 = f32[1024]{0:T(1024)S(1)} all-reduce(f32[1024]{0:T(1024)S(1)} %scatter_custom_fusion), channel_id=1, replica_groups=mesh['groups'=2,'edge'=4,'replica'=2,'probe'=2] {'edge'}, use_global_device_ids=true, to_apply=%region_7.10 | all-reduce | flops 1024 | bytes 8192 | tf_op jit(solution)/shard_map/psum | solution.py:84
  180.8 5.8 %gather_fusion.2 = f32[1536]{0:T(1024)S(1)} fusion(f32[1024]{0:T(1024)S(1)} %psum.67, s32[2048]{0:T(1024)S(1)} %pad_clamp_fusion.2), kind=kCustom, calls=%fused_computation.6 | custom fusion | bytes 18432 | tf_op jit(solution)/shard_map/jit(_take)/gather | solution.py:86
  186.7 2.4 fusion.27
  189.1 3.5 %fusion.15 = f32[256,256]{0,1:T(8,128)} fusion(bf16[256,128]{1,0:T(8,128)(2,1)} %param.27, f32[1536,256]{1,0:T(8,128)} %get-tuple-element.35, bf16[1,1536,256]{2,1,0:T(8,128)(2,1)} %param.17, f32[256]{0:T(256)S(1)} %convert_element_type.55, f32[1536]{0:T(1024)S(1)} %get-tuple-element.33, f32[128]{0:T(128)S(1)} %copy-done.9, f32[1536]{0:T(1024)S(1)} %broadcast_select_fusion), kind=kOutput, calls=%fused_computation.35 | convolution fusion | flops 306708480 | bytes 2700800 | tf_op jit(solution)/shard_map/dot_general | solution.py:92
  196.7 19.3 %all-reduce = (f32[256]{0:T(256)}, f32[128]{0:T(128)}) all-reduce(f32[256]{0:T(256)S(1)} %bitcast.76, f32[128]{0:T(128)S(1)} %convolution_bitcast_fusion.1), channel_id=1, replica_groups=mesh['groups'=2,'edge'=4,'replica'=2,'probe'=2] {'edge','replica'}, use_global_device_ids=true, to_apply=%region_10.13 | all-reduce | flops 384 | bytes 3072 | tf_op jit(solution)/shard_map/psum | solution.py:96
  216.0 46.5 %all-reduce.11.cloned.1.call-done = (f32[256,256]{0,1:T(8,128)}, f32[256,128]{1,0:T(8,128)}) async-done(((f32[256,256]{0,1:T(8,128)}, f32[256,128]{1,0:T(8,128)}), (f32[256,256]{0,1:T(8,128)}, f32[256,128]{1,0:T(8,128)})) %all-reduce.11.cloned.1.call-update) | async-done | bytes 393232 | tf_op jit(solution)/shard_map/psum | solution.py:96
  (74 shorter events, 25.9 us)
Async XLA Ops:
  7.2 25.3 %copy-start = (bf16[1,32,128,128]{3,2,1,0:T(8,128)(2,1)S(1)}, bf16[1,32,128,128]{3,2,1,0:T(8,128)(2,1)}, u32[]{:S(2)}) copy-start(bf16[1,32,128,128]{3,2,1,0:T(8,128)(2,1)} %param.21) | copy-start | bytes 3145732
  7.2 47.8 %all-reduce.7.cloned.1.call-start = ((), (), s32[]{:S(2)}) async-start(), calls=%async_computation | async-start | bytes 1048576 | tf_op jit(solution)/shard_map/psum | solution.py:54
  8.0 2.8 %copy-start.10 = (bf16[256,128]{1,0:T(8,128)(2,1)S(1)}, bf16[256,128]{1,0:T(8,128)(2,1)}, u32[]{:S(2)}) copy-start(bf16[256,128]{1,0:T(8,128)(2,1)} %param.27) | copy-start | bytes 196612
  10.9 2.9 %copy-start.2 = (bf16[1536,256]{1,0:T(8,128)(2,1)}, bf16[1536,256]{1,0:T(8,128)(2,1)S(1)}, u32[]{:S(2)}) copy-start(bf16[1536,256]{1,0:T(8,128)(2,1)S(1)} %get-tuple-element.34) | copy-start | bytes 2359300
  10.9 3.2 %copy-start.7 = (s32[1,1536]{1,0:T(1,128)S(1)}, s32[1,1536]{1,0:T(1,128)}, u32[]{:S(2)}) copy-start(s32[1,1536]{1,0:T(1,128)} %param.19) | copy-start | bytes 18436
  10.9 3.3 %copy-start.4 = (s32[3072,64]{0,1:T(8,128)S(1)}, s32[3072,64]{0,1:T(8,128)}, u32[]{:S(2)}) copy-start(s32[3072,64]{0,1:T(8,128)} %param.25) | copy-start | bytes 2359300
  13.8 124.2 %all-reduce.9.cloned.1.call-start = ((), (), s32[]{:S(2)}) async-start(), calls=%async_computation.1 | async-start | bytes 3145728 | tf_op jit(solution)/shard_map/psum | solution.py:75
  29.5 1.5 copy-start.5
  29.6 1.5 copy-start.12
  29.6 1.5 copy-start.11
  32.4 0.8 copy-start.8
  35.5 1.7 copy-start.6
  35.5 1.7 copy-start.3
  39.7 18.8 %copy-start.9 = (f32[128]{0:T(128)S(1)}, f32[128]{0:T(128)}, u32[]{:S(2)}) copy-start(f32[128]{0:T(128)} %param.29) | copy-start | bytes 1540
  68.7 193.7 %all-reduce.11.cloned.1.call-start = ((), (), s32[]{:S(2)}) async-start(), calls=%async_computation.2 | async-start | bytes 786432 | tf_op jit(solution)/shard_map/psum | solution.py:96
  153.1 2.6 copy-start.1
Sparse Core Ops, SparseCore 0:
  13.9 40.9 all-reduce.6
  68.8 69.0 all-reduce.8
  192.8 69.6 all-reduce.10
where the time goes:
time: 274 us; the launch traced here: 273 us
  waiting for transfers between devices  131 us (48%)
  local copies, waits for them, and re-layouts  46.3 us (17%)
  blocking collectives  32.2 us (12%)
  other arithmetic  26.4 us (10%)
  matrix products  20.8 us (8%)
  between operations  16.5 us (6%)
    psum x1, waiting for transfers between devices, body(): residual = lax.psum(model_part - ref_part, 'edge')  69 us
    psum x1, waiting for transfers between devices, body(): lax.psum((g_in, g_msg, g_stiff, g_env), ('edge', 'replica'))  46.5 us
    psum x1, blocking collectives, body(): lax.psum((g_in, g_msg, g_stiff, g_env), ('edge', 'replica'))  19.3 us
    psum x1, waiting for transfers between devices, body(): env = lax.psum(env_part, 'edge')  15.2 us
    scatter-add x1, other arithmetic, body(): weight = lax.psum(jax.ops.segment_sum(dzeta, recv, n_atoms), 'edge')  11.1 us
    psum x1, blocking collectives, body(): weight = lax.psum(jax.ops.segment_sum(dzeta, recv, n_atoms), 'edge')  9.83 us
    unnamed x32, local copies, waits for them, and re-layouts  6.39 us
    gather x1, local copies, waits for them, and re-layouts, body(): jnp.take(weight, recv, axis=0)[:, None] * w_env[None, :]  5.84 us
  transfers between devices with their start and end apart: 3, of which 3 were waited for; matrix products, arithmetic and copies ran while one was open for 10% of the time, Pallas kernels for 0%

commit v1 on v0

v1 whole, which is shorter than its diff:
```python
import functools

import jax
import jax.numpy as jnp
from jax import lax
from jax.experimental import pallas as pl
from jax.experimental.pallas import tpu as pltpu
from jax.sharding import PartitionSpec as P

TILE = 128
MESH = pl.DeviceIdType.MESH
F32 = jnp.float32
BF16 = jnp.bfloat16
NN = (((1,), (0,)), ((), ()))
NT = (((1,), (1,)), ((), ()))
TN = (((0,), (0,)), ((), ()))


def dot(a, b, dims=NN):
    return lax.dot_general(a, b, dims, preferred_element_type=F32)


def split(x, parts):
    out = []
    for _ in range(parts):
        piece = x.astype(BF16)
        out.append(piece)
        x = x - piece.astype(F32)
    return out


def stack_rows(rows):
    n = rows[0].shape[1]
    where = lax.broadcasted_iota(jnp.int32, (8, n), 0)
    out = jnp.zeros((8, n), F32)
    for i, row in enumerate(rows):
        out = jnp.where(where == i, row.astype(F32), out)
    return out.astype(BF16)


def row_dot(x, b, dims=NN, parts=3):
    return jnp.sum(dot(stack_rows(split(x, parts)), b, dims), axis=0, keepdims=True)


def sigmoid(x):
    return 1.0 / (1.0 + jnp.exp(-x))


def loop(count, fn):
    if count <= 16:
        for i in range(count):
            fn(i)
    else:
        def step(i, carry):
            fn(i)
            return carry
        lax.fori_loop(0, count, step, 0)


def tile_kernel(rows, cols, count, tiles, probes, pt_ref, ref_ref, pb, pf, acc):
    n_slots = tiles.shape[1]
    atoms = pt_ref.shape[1]
    share = probes.shape[1]
    pv = probes[...].astype(F32)
    pf[:, :share] = pv
    pb[...] = pv.astype(BF16).reshape(pb.shape)
    acc[...] = jnp.zeros_like(acc)
    live = count[0, 0]
    unroll = 8 if n_slots % 8 == 0 else 1

    def step(i, carry):
        for j in range(unroll):
            t = i * unroll + j
            prod = dot(tiles[0, t], pb[cols[0, t]])
            prod = jnp.where(t < live, prod, 0.0)
            at = pl.ds(pl.multiple_of(rows[0, t] * TILE, TILE), TILE)
            acc[at, :share] += prod
        return carry

    lax.fori_loop(0, (live + unroll - 1) // unroll, step, 0)
    for c in range(3):
        pick = pl.ds(c, atoms, stride=3)
        pt_ref[c * share:(c + 1) * share, :] = pf[pick, :].T[:share].astype(BF16)
        ref_ref[c * share:(c + 1) * share, :] = acc[pick, :].T[:share]


def main_kernel(
    n_e, n_r, n_p, probes_total,
    feats, vecs, send, recv, pt, refs, w_in, w_msg, w_stiff, w_env,
    res_out, mse_out, gin_out, gmsg_out, gstiff_out, genv_out,
    hot_r, hot_s, pre, latent, proj, contrib, rd,
    s_buf, part_buf, got_buf, r_buf, w_buf, z_buf, g_buf, gg_buf, gf_buf, v_buf,
    s_ss, s_rs, rs_ss, rs_rs, ag_ss, ag_rs, w_ss, w_rs, z_ss, z_rs, g_ss, g_rs, gf_ss, gf_rs, v_ss, v_rs,
):
    edges = send.shape[1]
    atoms = pt.shape[1]
    share = pt.shape[0] // 3
    width = w_in.shape[1]
    half = width // n_p
    own_n, piece = r_buf.shape[0], r_buf.shape[2]
    lanes = 256
    me_e, me_r, me_p = lax.axis_index("edge"), lax.axis_index("replica"), lax.axis_index("probe")

    def dev(e, r, p):
        return {"edge": e, "replica": r, "probe": p}

    def copy(src, dst, ss, rs, device):
        return pltpu.make_async_remote_copy(
            src_ref=src, dst_ref=dst, send_sem=ss, recv_sem=rs, device_id=device, device_id_type=MESH)

    barrier = pltpu.get_barrier_semaphore()
    n_all = n_e * n_r * n_p
    me_all = (me_e * n_r + me_r) * n_p + me_p

    def all_dev(f):
        return dev(f // (n_r * n_p), (f // n_p) % n_r, f % n_p)

    def greet(i):
        pl.semaphore_signal(barrier, inc=1, device_id=all_dev((me_all + i + 1) % n_all), device_id_type=MESH)

    loop(n_all - 1, greet)

    def spread(buf, ss, rs, me, n, device):
        def go(i):
            copy(buf.at[me], buf.at[me], ss.at[i], rs.at[me], device((me + i + 1) % n)).start()
        loop(n - 1, go)

    def gathered(buf, ss, rs, me, n, device):
        def go(i):
            j = (me + i + 1) % n
            c = copy(buf.at[j], buf.at[j], ss.at[i], rs.at[j], device(j))
            c.wait_recv()
            c.wait_send()
        loop(n - 1, go)

    def total(buf, n):
        if n <= 16:
            out = buf[0]
            for j in range(1, n):
                out = out + buf[j]
            return out
        return lax.fori_loop(1, n, lambda j, t: t + buf[j], buf[0])

    wenv = w_env[...]
    u = row_dot(wenv, w_msg[...], NT)
    u_hi, u_lo = split(u, 2)
    readout = stack_rows([w_stiff[...], u_hi, u_lo])
    rows = 256 if edges % 256 == 0 else edges

    def forward(i, carry):
        at = pl.ds(pl.multiple_of(i * rows, rows), rows)
        x = dot(feats[0, at, :], w_in[...])
        for p in range(n_p):
            pre[p, at, :] = x[:, p * half:(p + 1) * half]
        latent[at, :] = (x * sigmoid(x)).astype(BF16)
        return carry

    lax.fori_loop(0, edges // rows, forward, 0)

    snd, rcv = send[...], recv[...]

    def hots(i, carry):
        base = i * 32
        ids = lax.broadcasted_iota(jnp.int32, (32, edges), 0) + base
        at = pl.ds(pl.multiple_of(base, 32), 32)
        r = jnp.where(ids == rcv, 1.0, 0.0)
        s = jnp.where(ids == snd, 1.0, 0.0)
        hot_r[at, :] = r.astype(BF16)
        hot_s[at, :] = (s - r).astype(BF16)
        return carry

    lax.fori_loop(0, atoms // 32, hots, 0)
    read = dot(readout, latent[...], NT)
    lw = read[0:1]
    mw = read[1:2] + read[2:3]
    s_buf[me_e] = row_dot(mw, hot_r[...], NT)
    pl.semaphore_wait(barrier, n_all - 1)
    edge_dev = lambda e: dev(e, me_r, me_p)
    spread(s_buf, s_ss, s_rs, me_e, n_e, edge_dev)

    vec = [vecs[0, c:c + 1, :] for c in range(3)]

    def project(i, carry):
        at = pl.ds(pl.multiple_of(i * lanes, lanes), lanes)
        delta = dot(pt[...], hot_s[:, at])
        v = vecs[0, :, at]
        out = v[0:1] * delta[:share]
        for c in (1, 2):
            out = out + v[c:c + 1] * delta[c * share:(c + 1) * share]
        proj[:, at] = out
        return carry

    lax.fori_loop(0, edges // lanes, project, 0)
    gathered(s_buf, s_ss, s_rs, me_e, n_e, edge_dev)
    zeta = lw + row_dot(total(s_buf, n_e), hot_r[...])
    stiff = jnp.maximum(zeta, 0.0) + jnp.log1p(jnp.exp(-jnp.abs(zeta)))
    sig_z = sigmoid(zeta)
    for c in range(3):
        contrib[c * share:(c + 1) * share, :] = (stiff * vec[c] * proj[...]).astype(BF16)

    def model(q):
        at = pl.ds(pl.multiple_of(q * piece, piece), piece)
        return dot(contrib[...], hot_s[at, :], NT) - refs[:, at]

    def rs_copy(i, q, src):
        return copy(part_buf.at[q], got_buf.at[src], rs_ss.at[i], rs_rs.at[src], edge_dev(q))

    def send_piece(i):
        q = (me_e + i + 1) % n_e

        def go():
            part_buf[q] = model(q)
            rs_copy(i, q, me_e).start()

        if own_n == n_e:
            go()
        else:
            pl.when(q < own_n)(go)

    loop(n_e - 1, send_piece)

    def own():
        got_buf[me_e] = model(me_e)

        def wait(i):
            j = (me_e + i + 1) % n_e
            copy(got_buf.at[j], got_buf.at[j], rs_ss.at[i], rs_rs.at[j], edge_dev(j)).wait_recv()

        loop(n_e - 1, wait)
        r_buf[me_e] = total(got_buf, n_e)

        def give(i):
            q = (me_e + i + 1) % n_e
            copy(r_buf.at[me_e], r_buf.at[me_e], ag_ss.at[i], ag_rs.at[me_e], edge_dev(q)).start()

        loop(n_e - 1, give)

    if own_n == n_e:
        own()
    else:
        pl.when(me_e < own_n)(own)

    rd[...] = jnp.zeros_like(rd)

    def use(q, square):
        r = r_buf[q]
        hi, lo = split(r, 2)
        both = jnp.concatenate([hi, lo], axis=0)
        at = pl.ds(pl.multiple_of(q * piece, piece), piece)
        for i in range(edges // lanes):
            cut = slice(i * lanes, (i + 1) * lanes)
            x = dot(both, hot_s[at, cut])
            rd[:, cut] += x[:3 * share] + x[3 * share:]
        return square + jnp.sum(jnp.sum(r * r, axis=0, keepdims=True), axis=1, keepdims=True)

    square = jnp.zeros((1, 1), F32)
    for i in range(n_e):
        q = (me_e + i) % n_e
        if i:
            def wait(q=q):
                copy(r_buf.at[q], r_buf.at[q], ag_ss.at[0], ag_rs.at[q], edge_dev(q)).wait_recv()
            if own_n == n_e:
                wait()
            else:
                pl.when(q < own_n)(wait)
        if own_n == n_e:
            square = use(q, square)
    if own_n != n_e:
        square = lax.fori_loop(0, own_n, use, square)

    rproj = vec[0] * rd[:share]
    for c in (1, 2):
        rproj = rproj + vec[c] * rd[c * share:(c + 1) * share]
    dst = (2.0 / probes_total) * jnp.sum(proj[...] * rproj, axis=0, keepdims=True)
    dz_part = dst * sig_z
    n_w = n_e * n_p
    me_w = me_e * n_p + me_p
    w_dev = lambda f: dev(f // n_p, me_r, f % n_p)
    p_dev = lambda p: dev(me_e, me_r, p)
    w_buf[me_w, :, :atoms] = row_dot(dz_part, hot_r[...], NT)
    w_buf[me_w, :, atoms:] = jnp.broadcast_to(square, (1, 128))
    z_buf[me_p] = dz_part
    spread(w_buf, w_ss, w_rs, me_w, n_w, w_dev)
    spread(z_buf, z_ss, z_rs, me_p, n_p, p_dev)

    for q in range(own_n):
        for c in range(3):
            x = r_buf[q, c * share:(c + 1) * share, :]
            res_out[pl.ds(q * piece * 3 + c, piece, stride=3), :] = x.T

    gathered(w_buf, w_ss, w_rs, me_w, n_w, w_dev)
    gathered(z_buf, z_ss, z_rs, me_p, n_p, p_dev)
    weight = total(w_buf, n_w)[:, :atoms]
    squares = w_buf[me_e * n_p, :, atoms:]
    for p in range(1, n_p):
        squares = squares + w_buf[me_e * n_p + p, :, atoms:]
    mse_out[...] = squares / (3 * atoms * probes_total)
    dz = total(z_buf, n_p)
    wr = row_dot(weight, hot_r[...])

    dz_hi, dz_lo = split(dz, 2)
    wr_hi, wr_lo = split(wr, 2)
    sums = dot(stack_rows([dz_hi, dz_lo, wr_hi, wr_lo]), latent[...])
    g_members = n_e * n_r
    me_g = me_e * n_r + me_r
    g_dev = lambda f: dev(f // n_r, f % n_r, me_p)
    v_buf[me_g] = jnp.zeros(v_buf.shape[1:], F32)
    v_buf[me_g, 0:1] = sums[0:1] + sums[1:2]
    v_buf[me_g, 1:2] = sums[2:3] + sums[3:4]
    spread(v_buf, v_ss, v_rs, me_g, g_members, g_dev)

    ws = w_stiff[...].astype(F32)
    ws_half = ws[:, :half]
    u_half = u[:, :half]
    for p in range(1, n_p):
        ws_half = jnp.where(me_p == p, ws[:, p * half:(p + 1) * half], ws_half)
        u_half = jnp.where(me_p == p, u[:, p * half:(p + 1) * half], u_half)
    uh_hi, uh_lo = split(u_half, 2)
    dlat = dot(
        stack_rows([dz_hi, dz_lo, wr_hi, wr_hi, wr_lo]),
        stack_rows([ws_half, ws_half, uh_hi, uh_lo, uh_hi]), TN)
    x = pre[me_p]
    sg = sigmoid(x)
    dpre = (dlat * sg * (1.0 + x * (1.0 - sg))).astype(BF16)
    g_half = dot(feats[0], dpre, TN)
    g_own, g_rows = gf_buf.shape[1], gf_buf.shape[2]
    g_buf[...] = g_half.reshape(g_buf.shape)

    def g_send(i):
        q = (me_g + i + 1) % g_members

        def go():
            copy(g_buf.at[q], gg_buf.at[me_g], g_ss.at[i], g_rs.at[me_g], g_dev(q)).start()

        if g_own == g_members:
            go()
        else:
            pl.when(q < g_own)(go)

    loop(g_members - 1, g_send)

    def gf_copy(i, g, p, f):
        return copy(gf_buf.at[p, g], gf_buf.at[p, g], gf_ss.at[i], gf_rs.at[p, g], all_dev(f))

    def g_own_part():
        gg_buf[me_g] = g_buf[me_g]

        def wait(i):
            j = (me_g + i + 1) % g_members
            copy(gg_buf.at[j], gg_buf.at[j], g_ss.at[i], g_rs.at[j], g_dev(j)).wait_recv()

        loop(g_members - 1, wait)
        gf_buf[me_p, me_g] = total(gg_buf, g_members)

        def give(i):
            gf_copy(i, me_g, me_p, (me_all + i + 1) % n_all).start()

        loop(n_all - 1, give)

    if g_own == g_members:
        g_own_part()
    else:
        pl.when(me_g < g_own)(g_own_part)

    gathered(v_buf, v_ss, v_rs, me_g, g_members, g_dev)
    v = total(v_buf, g_members)
    gstiff_out[...] = v[0:1]
    q_row = v[1:2]
    q_hi, q_lo = split(q_row, 2)
    e_hi, e_lo = split(wenv, 2)
    gmsg_out[...] = dot(stack_rows([q_hi, q_hi, q_lo]), stack_rows([e_hi, e_lo, e_hi]), TN)
    genv_out[...] = row_dot(q_row, w_msg[...])

    def g_arrive(i):
        f = (me_all + i + 1) % n_all
        p, g = f % n_p, f // n_p

        def go():
            gf_copy(i, g, p, f).wait_recv()

        if g_own == g_members:
            go()
        else:
            pl.when(g < g_own)(go)

    loop(n_all - 1, g_arrive)
    for p in range(n_p):
        gin_out[:, p * half:(p + 1) * half] = gf_buf[p].reshape(width, half)

    def sent(i):
        q = (me_e + i + 1) % n_e

        def go():
            rs_copy(i, q, me_e).wait_send()

        if own_n == n_e:
            go()
        else:
            pl.when(q < own_n)(go)

    loop(n_e - 1, sent)

    def ag_sent():
        loop(n_e - 1, lambda i: copy(
            r_buf.at[me_e], r_buf.at[me_e], ag_ss.at[i], ag_rs.at[me_e], edge_dev((me_e + i + 1) % n_e)).wait_send())

    if own_n == n_e:
        ag_sent()
    else:
        pl.when(me_e < own_n)(ag_sent)

    def g_sent(i):
        q = (me_g + i + 1) % g_members

        def go():
            copy(g_buf.at[q], gg_buf.at[me_g], g_ss.at[i], g_rs.at[me_g], g_dev(q)).wait_send()

        if g_own == g_members:
            go()
        else:
            pl.when(q < g_own)(go)

    loop(g_members - 1, g_sent)

    def gf_sent():
        loop(n_all - 1, lambda i: gf_copy(i, me_g, me_p, (me_all + i + 1) % n_all).wait_send())

    if g_own == g_members:
        gf_sent()
    else:
        pl.when(me_g < g_own)(gf_sent)


def body(
    n_e, n_r, n_p,
    edge_feats, edge_vecs, senders, receivers, tiles, tile_rows, tile_cols, tile_count,
    probes, w_in, w_msg, w_stiff, w_env,
):
    share = probes.shape[1]
    dim = probes.shape[0]
    atoms = dim // 3
    edges = senders.shape[1]
    width = w_in.shape[1]
    msg = w_msg.shape[1]
    vm = pl.BlockSpec(memory_space=pltpu.VMEM)
    sm = pl.BlockSpec(memory_space=pltpu.SMEM)
    pt, refs = pl.pallas_call(
        tile_kernel,
        out_shape=(
            jax.ShapeDtypeStruct((3 * share, atoms), BF16),
            jax.ShapeDtypeStruct((3 * share, atoms), F32),
        ),
        in_specs=[sm, sm, sm, vm, vm],
        out_specs=(vm, vm),
        scratch_shapes=[
            pltpu.VMEM((dim // TILE, TILE, share), BF16),
            pltpu.VMEM((dim, 128), F32),
            pltpu.VMEM((dim, 128), F32),
        ],
        compiler_params=pltpu.CompilerParams(vmem_limit_bytes=40 * 2**20),
        name="tiles",
    )(tile_rows, tile_cols, tile_count, tiles, probes)

    own_n = min(n_e, atoms // 128)
    piece = atoms // own_n
    g_members = n_e * n_r
    g_own = min(g_members, width // 8)
    g_rows = width // g_own
    half = width // n_p
    n_all = n_e * n_r * n_p
    n_w = n_e * n_p
    sem = lambda *shape: pltpu.SemaphoreType.DMA(shape)
    vmem = pltpu.VMEM
    outs = pl.pallas_call(
        functools.partial(main_kernel, n_e, n_r, n_p, share * n_p),
        out_shape=(
            jax.ShapeDtypeStruct((dim, share), F32),
            jax.ShapeDtypeStruct((1, 128), F32),
            jax.ShapeDtypeStruct((width, width), F32),
            jax.ShapeDtypeStruct((width, msg), F32),
            jax.ShapeDtypeStruct((1, width), F32),
            jax.ShapeDtypeStruct((1, msg), F32),
        ),
        in_specs=[vm] * 10,
        out_specs=(vm,) * 6,
        scratch_shapes=[
            vmem((atoms, edges), BF16),
            vmem((atoms, edges), BF16),
            vmem((n_p, edges, half), F32),
            vmem((edges, width), BF16),
            vmem((share, edges), F32),
            vmem((3 * share, edges), BF16),
            vmem((3 * share, edges), F32),
            vmem((n_e, 1, atoms), F32),
            vmem((own_n, 3 * share, piece), F32),
            vmem((n_e, 3 * share, piece), F32),
            vmem((own_n, 3 * share, piece), F32),
            vmem((n_w, 1, atoms + 128), F32),
            vmem((n_p, 1, edges), F32),
            vmem((g_own, g_rows, half), F32),
            vmem((g_members, g_rows, half), F32),
            vmem((n_p, g_own, g_rows, half), F32),
            vmem((g_members, 8, width), F32),
            sem(n_e), sem(n_e),
            sem(n_e), sem(n_e),
            sem(n_e), sem(n_e),
            sem(n_w), sem(n_w),
            sem(n_p), sem(n_p),
            sem(g_members), sem(g_members),
            sem(n_all), sem(n_p, g_members),
            sem(g_members), sem(g_members),
        ],
        compiler_params=pltpu.CompilerParams(
            collective_id=0, has_side_effects=True, vmem_limit_bytes=48 * 2**20),
        name="edges",
    )(
        edge_feats, edge_vecs, senders, receivers, pt, refs, w_in, w_msg,
        w_stiff.reshape(1, -1), w_env.reshape(1, -1),
    )
    residual, mse, g_in, g_msg, g_stiff, g_env = outs
    return (residual[None], mse[0, :1], g_in, g_msg, g_stiff[0], g_env[0])


def solution(mesh):
    n_e, n_r, n_p = mesh.shape["edge"], mesh.shape["replica"], mesh.shape["probe"]
    return jax.shard_map(
        functools.partial(body, n_e, n_r, n_p),
        mesh=mesh,
        in_specs=(
            P(("groups", "replica"), "edge", None),
            P(("groups", "replica"), None, "edge"),
            P(("groups", "replica"), "edge"),
            P(("groups", "replica"), "edge"),
            P(("groups", "replica"), "edge", None, None),
            P(("groups", "replica"), "edge"),
            P(("groups", "replica"), "edge"),
            P(("groups", "replica"), "edge"),
            P(None, "probe"),
            P(),
            P(),
            P(),
            P(),
        ),
        out_specs=(
            P(("groups", "replica"), None, "probe"),
            P(("groups", "replica")),
            P("groups", None),
            P("groups", None),
            P("groups"),
            P("groups"),
        ),
        check_vma=False,
    )
```

time: 274 us -> 79.5 us (0.29)
  waiting for transfers between devices: 131 us -> 0 us
  Pallas kernels: 0 us -> 69.6 us
  local copies, waits for them, and re-layouts: 46.3 us -> 6.8 us
  blocking collectives: 32.2 us -> 0 us
  other arithmetic: 26.4 us -> 0 us
  matrix products: 20.8 us -> 0 us
  between operations: 16.5 us -> 2.71 us
    psum x3 -> x0, waiting for transfers between devices: 131 us -> none  [the longest x1 69 us: body(): residual = lax.psum(model_part - ref_part, 'edge')]
    pallas_call x0 -> x2, Pallas kernels: none -> 69.6 us  [the longest x1 67.6 us: body(): pl.pallas_call(functools.partial(main_kernel, n_e, n_r, n_p, share * n_p)...]
    psum x3 -> x0, blocking collectives: 32.2 us -> none  [the longest x1 19.3 us: body(): lax.psum((g_in, g_msg, g_stiff, g_env), ('edge', 'replica'))]
    gather x7 -> x0, local copies, waits for them, and re-layouts: 28.8 us -> none  [the longest x1 5.84 us: body(): jnp.take(weight, recv, axis=0)[:, None] * w_env[None, :]]
    dot_general x11 -> x0, matrix products: 20.8 us -> none  [the longest x1 3.53 us: body(): lax.dot_general(feats, dpre, contract, preferred_element_type=jnp.float32)]
    scatter-add x1 -> x0, other arithmetic: 11.1 us -> none  [body(): weight = lax.psum(jax.ops.segment_sum(dzeta, recv, n_atoms), 'edge')]
    reshape x4 -> x1, local copies, waits for them, and re-layouts: 8.15 us -> 0.66 us  [body(): w_stiff.reshape(1, -1)]
    sub x2 -> x0, other arithmetic: 5.05 us -> none  [the longest x1 2.69 us: body(): residual = lax.psum(model_part - ref_part, 'edge')]
  transfers between devices with their start and end apart: 3 -> 0, of which waited for: 3 -> 0; matrix products, arithmetic and copies ran while one was open for 10% -> 0% of each run, Pallas kernels for 0% -> 0%
where the time goes in v1:
time: 79.5 us; the launch traced here: 79.1 us
  Pallas kernels  69.6 us (88%)
  local copies, waits for them, and re-layouts  6.8 us (9%)
  between operations  2.71 us (3%)
    pallas_call x1, Pallas kernels, body(): pl.pallas_call(functools.partial(main_kernel, n_e, n_r, n_p, share * n_p)...  67.6 us
    unnamed x25, local copies, waits for them, and re-layouts  6.14 us
    pallas_call x1, Pallas kernels, body(): pl.pallas_call(tile_kernel, out_shape=(jax.ShapeDtypeStruct((3 * share, a...  2.04 us

profile of v1, /device:TPU:0, one launch (start us, length us, event | category | flops | bytes accessed | tf_op | source)
XLA Modules:
  0.0 79.1 jit_solution(6598703706385170577)
XLA Ops:
  0.6 0.0 copy-start.8
  0.6 0.0 copy-start.7
  0.7 0.0 copy-start
  1.4 0.7 reshape.18.w_stiff
  2.1 0.7 copy.20.vecs
  2.8 1.6 %copy.19.probes = s32[3072,64]{1,0:T(8,128)S(1)} copy(s32[3072,64]{0,1:T(8,128)} %param.21) | data formatting | bytes 1572864 | tf_op args[8]
  4.4 0.0 copy-done.8
  4.4 0.0 copy-done.7
  4.4 0.0 copy-done
  4.4 0.0 copy-start.1
  4.4 0.0 copy-start.2
  4.4 0.0 copy-start.3
  4.5 0.0 copy-start.4
  4.5 0.0 copy-start.5
  4.5 0.0 copy-start.6
  4.5 2.0 %tiles.2 = (bf16[192,1024]{1,0:T(8,128)(2,1)S(1)}, f32[192,1024]{1,0:T(8,128)S(1)}) custom-call(s32[1,32]{1,0:T(1,128)S(1)} %copy-done.7, s32[1,32]{1,0:T(1,128)S(1)} %copy-done.8, s32[1,1]{1,0:T(1,128)S(6)} %copy.27.count, bf16[1,32,128,128]{3,2,1,0:T(8,128)(2,1)S(1)} %copy-done, s32[3072,64]{1,0:T(8,128)S(1)} %copy.19.probes), custom_call_target="tpu_custom_call" | custom-call | tf_op jit(solution)/shard_map/tiles/pallas_call | solution.py:447
  6.5 0.0 copy-done.1
  6.5 0.0 copy-done.2
  6.6 67.6 %edges.1 = (f32[3072,64]{1,0:T(8,128)S(1)}, f32[1,128]{1,0:T(1,128)S(1)}, f32[256,256]{1,0:T(8,128)S(1)}, f32[256,128]{1,0:T(8,128)S(1)}, f32[1,256]{1,0:T(1,128)S(1)}, /*index=5*/f32[1,128]{1,0:T(1,128)S(1)}) custom-call(bf16[1,1536,256]{2,1,0:T(8,128)(2,1)S(1)} %copy-done.1, f32[1,3,1536]{2,1,0:T(4,128)S(1)} %copy.20.vecs, s32[1,1536]{1,0:T(1,128)S(1)} %copy-done.4, ...), custom_call_target="tpu_custom_call" | custom-call | tf_op jit(solution)/shard_map/edges/pallas_call | solution.py:474
  74.2 1.3 %copy.21 = f32[1,3072,64]{1,2,0:T(8,128)} copy(f32[1,3072,64]{2,1,0:T(8,128)S(1)} %bitcast.6) | data formatting | bytes 1572864
  75.5 0.7 copy.29
  76.2 0.7 copy.30
  76.9 0.6 copy.31
  77.5 0.5 copy.32
  (4 shorter events, 0.0 us)
Async XLA Ops:
  0.6 3.8 %copy-start.8 = (s32[1,32]{1,0:T(1,128)S(1)}, s32[1,32]{1,0:T(1,128)}, u32[]{:S(2)}) copy-start(s32[1,32]{1,0:T(1,128)} %cols.1) | copy-start | bytes 388
  0.6 3.8 %copy-start.7 = (s32[1,32]{1,0:T(1,128)S(1)}, s32[1,32]{1,0:T(1,128)}, u32[]{:S(2)}) copy-start(s32[1,32]{1,0:T(1,128)} %rows.1) | copy-start | bytes 388
  0.7 3.8 %copy-start = (bf16[1,32,128,128]{3,2,1,0:T(8,128)(2,1)S(1)}, bf16[1,32,128,128]{3,2,1,0:T(8,128)(2,1)}, u32[]{:S(2)}) copy-start(bf16[1,32,128,128]{3,2,1,0:T(8,128)(2,1)} %tiles.3) | copy-start | bytes 3145732
  4.4 2.1 %copy-start.1 = (bf16[1,1536,256]{2,1,0:T(8,128)(2,1)S(1)}, bf16[1,1536,256]{2,1,0:T(8,128)(2,1)}, u32[]{:S(2)}) copy-start(bf16[1,1536,256]{2,1,0:T(8,128)(2,1)} %feats.1) | copy-start | bytes 2359300
  4.4 2.1 %copy-start.2 = (bf16[256,256]{1,0:T(8,128)(2,1)S(1)}, bf16[256,256]{1,0:T(8,128)(2,1)}, u32[]{:S(2)}) copy-start(bf16[256,256]{1,0:T(8,128)(2,1)} %w_in.1) | copy-start | bytes 393220
  4.4 2.1 %copy-start.3 = (bf16[256,128]{1,0:T(8,128)(2,1)S(1)}, bf16[256,128]{1,0:T(8,128)(2,1)}, u32[]{:S(2)}) copy-start(bf16[256,128]{1,0:T(8,128)(2,1)} %w_msg.1) | copy-start | bytes 196612
  4.5 2.1 %copy-start.4 = (s32[1,1536]{1,0:T(1,128)S(1)}, s32[1,1536]{1,0:T(1,128)}, u32[]{:S(2)}) copy-start(s32[1,1536]{1,0:T(1,128)} %send.1) | copy-start | bytes 18436
  4.5 2.1 %copy-start.5 = (s32[1,1536]{1,0:T(1,128)S(1)}, s32[1,1536]{1,0:T(1,128)}, u32[]{:S(2)}) copy-start(s32[1,1536]{1,0:T(1,128)} %recv.1) | copy-start | bytes 18436
  4.5 2.1 %copy-start.6 = (f32[128]{0:T(128)S(1)}, f32[128]{0:T(128)}, u32[]{:S(2)}) copy-start(f32[128]{0:T(128)} %param.25) | copy-start | bytes 1540

commit v2 on v1

--- a/solution.py
+++ b/solution.py
@@ -89,8 +89,8 @@
     feats, vecs, send, recv, pt, refs, w_in, w_msg, w_stiff, w_env,
     res_out, mse_out, gin_out, gmsg_out, gstiff_out, genv_out,
     hot_r, hot_s, pre, latent, proj, contrib, rd,
-    s_buf, part_buf, got_buf, r_buf, w_buf, z_buf, g_buf, gg_buf, gf_buf, v_buf,
-    s_ss, s_rs, rs_ss, rs_rs, ag_ss, ag_rs, w_ss, w_rs, z_ss, z_rs, g_ss, g_rs, gf_ss, gf_rs, v_ss, v_rs,
+    s_buf, part_buf, got_buf, y_buf, r_buf, w_buf, z_buf, g_buf, gg_buf, gf_buf, v_buf,
+    s_ss, s_rs, rs_ss, rs_rs, y_ss, y_rs, ag_ss, ag_rs, w_ss, w_rs, z_ss, z_rs, g_ss, g_rs, gf_ss, gf_rs, v_ss, v_rs,
 ):
     edges = send.shape[1]
     atoms = pt.shape[1]
@@ -198,75 +198,170 @@
     for c in range(3):
         contrib[c * share:(c + 1) * share, :] = (stiff * vec[c] * proj[...]).astype(BF16)
 
-    def model(q):
-        at = pl.ds(pl.multiple_of(q * piece, piece), piece)
-        return dot(contrib[...], hot_s[at, :], NT) - refs[:, at]
-
-    def rs_copy(i, q, src):
-        return copy(part_buf.at[q], got_buf.at[src], rs_ss.at[i], rs_rs.at[src], edge_dev(q))
-
-    def send_piece(i):
-        q = (me_e + i + 1) % n_e
-
-        def go():
-            part_buf[q] = model(q)
-            rs_copy(i, q, me_e).start()
+    def tree():
+        chunks = r_buf.shape[0]
+        near = edge_dev(me_e + 1 - 2 * (me_e % 2))
+        across = edge_dev(3 - me_e)
+        middle = (me_e == 1) | (me_e == 2)
+        is_end = (me_e == 0) | (me_e == 3)
+
+        def inward(k):
+            return copy(part_buf.at[k], got_buf.at[k], rs_ss.at[k], rs_rs.at[k], near)
+
+        def over(k):
+            return copy(part_buf.at[k], y_buf.at[k], y_ss.at[k], y_rs.at[k], across)
+
+        def outward(k):
+            return copy(r_buf.at[k], r_buf.at[k], ag_ss.at[k], ag_rs.at[k], near)
+
+        for k in range(0, chunks, 2):
+            at = slice(k * 128, k * 128 + 256)
+            m = dot(contrib[...], hot_s[at, :], NT) - refs[:, at]
+            part_buf[k] = m[:, :128]
+            part_buf[k + 1] = m[:, 128:]
+
+            @pl.when(is_end)
+            def _(k=k):
+                inward(k).start()
+                inward(k + 1).start()
+
+        square = jnp.zeros((1, 1), F32)
+        for k in range(chunks + 1):
+            @pl.when(middle)
+            def _(k=k):
+                if k < chunks:
+                    inward(k).wait_recv()
+                    part_buf[k] += got_buf[k]
+                    over(k).start()
+                if k:
+                    over(k - 1).wait_recv()
+                    r_buf[k - 1] = part_buf[k - 1] + y_buf[k - 1]
+                    outward(k - 1).start()
+
+            if k:
+                @pl.when(is_end)
+                def _(k=k):
+                    outward(k - 1).wait_recv()
+
+            if k and k % 2 == 0:
+                r = jnp.concatenate([r_buf[k - 2], r_buf[k - 1]], axis=1)
+                hi, lo = split(r, 2)
+                both = jnp.concatenate([hi, lo], axis=0)
+                for i in range(edges // lanes):
+                    cut = slice(i * lanes, (i + 1) * lanes)
+                    x = dot(both, hot_s[(k - 2) * 128:k * 128, cut])
+                    rd[:, cut] += x[:3 * share] + x[3 * share:]
+                square = square + jnp.sum(jnp.sum(r * r, axis=0, keepdims=True), axis=1, keepdims=True)
+
+        @pl.when(is_end)
+        def _():
+            for k in range(chunks):
+                inward(k).wait_send()
+
+        @pl.when(middle)
+        def _():
+            for k in range(chunks):
+                over(k).wait_send()
+                outward(k).wait_send()
+
+        return square
+
+    def direct():
+        def model(q):
+            at = pl.ds(pl.multiple_of(q * piece, piece), piece)
+            return dot(contrib[...], hot_s[at, :], NT) - refs[:, at]
+
+        def rs_copy(i, q, src):
+            return copy(part_buf.at[q], got_buf.at[src], rs_ss.at[i], rs_rs.at[src], edge_dev(q))
+
+        def send_piece(i):
+            q = (me_e + i + 1) % n_e
+
+            def go():
+                part_buf[q] = model(q)
+                rs_copy(i, q, me_e).start()
+
+            if own_n == n_e:
+                go()
+            else:
+                pl.when(q < own_n)(go)
+
+        loop(n_e - 1, send_piece)
+
+        def own():
+            got_buf[me_e] = model(me_e)
+
+            def wait(i):
+                j = (me_e + i + 1) % n_e
+                copy(got_buf.at[j], got_buf.at[j], rs_ss.at[i], rs_rs.at[j], edge_dev(j)).wait_recv()
+
+            loop(n_e - 1, wait)
+            r_buf[me_e] = total(got_buf, n_e)
+
+            def give(i):
+                q = (me_e + i + 1) % n_e
+                copy(r_buf.at[me_e], r_buf.at[me_e], ag_ss.at[i], ag_rs.at[me_e], edge_dev(q)).start()
+
+            loop(n_e - 1, give)
 
         if own_n == n_e:
-            go()
+            own()
         else:
-            pl.when(q < own_n)(go)
-
-    loop(n_e - 1, send_piece)
-
-    def own():
-        got_buf[me_e] = model(me_e)
-
-        def wait(i):
-            j = (me_e + i + 1) % n_e
-            copy(got_buf.at[j], got_buf.at[j], rs_ss.at[i], rs_rs.at[j], edge_dev(j)).wait_recv()
-
-        loop(n_e - 1, wait)
-        r_buf[me_e] = total(got_buf, n_e)
-
-        def give(i):
+            pl.when(me_e < own_n)(own)
+
+        def use(q, square):
+            r = r_buf[q]
+            hi, lo = split(r, 2)
+            both = jnp.concatenate([hi, lo], axis=0)
+            at = pl.ds(pl.multiple_of(q * piece, piece), piece)
+            for i in range(edges // lanes):
+                cut = slice(i * lanes, (i + 1) * lanes)
+                x = dot(both, hot_s[at, cut])
+                rd[:, cut] += x[:3 * share] + x[3 * share:]
+            return square + jnp.sum(jnp.sum(r * r, axis=0, keepdims=True), axis=1, keepdims=True)
+
+        square = jnp.zeros((1, 1), F32)
+        for i in range(n_e):
+            q = (me_e + i) % n_e
+            if i:
+                def wait(q=q):
+                    copy(r_buf.at[q], r_buf.at[q], ag_ss.at[0], ag_rs.at[q], edge_dev(q)).wait_recv()
+                if own_n == n_e:
+                    wait()
+                else:
+                    pl.when(q < own_n)(wait)
+            if own_n == n_e:
+                square = use(q, square)
+        if own_n != n_e:
+            square = lax.fori_loop(0, own_n, use, square)
+        def sent(i):
             q = (me_e + i + 1) % n_e
-            copy(r_buf.at[me_e], r_buf.at[me_e], ag_ss.at[i], ag_rs.at[me_e], edge_dev(q)).start()
-
-        loop(n_e - 1, give)
-
-    if own_n == n_e:
-        own()
+
+            def go():
+                rs_copy(i, q, me_e).wait_send()
+
+            if own_n == n_e:
+                go()
+            else:
+                pl.when(q < own_n)(go)
+
+        loop(n_e - 1, sent)
+
+        def ag_sent():
+            loop(n_e - 1, lambda i: copy(
+                r_buf.at[me_e], r_buf.at[me_e], ag_ss.at[i], ag_rs.at[me_e], edge_dev((me_e + i + 1) % n_e)).wait_send())
+
+        if own_n == n_e:
+            ag_sent()
+        else:
+            pl.when(me_e < own_n)(ag_sent)
+        return square
+
+    rd[...] = jnp.zeros_like(rd)
+    if n_e == 4:
+        square = tree()
     else:
-        pl.when(me_e < own_n)(own)
-
-    rd[...] = jnp.zeros_like(rd)
-
-    def use(q, square):
-        r = r_buf[q]
-        hi, lo = split(r, 2)
-        both = jnp.concatenate([hi, lo], axis=0)
-        at = pl.ds(pl.multiple_of(q * piece, piece), piece)
-        for i in range(edges // lanes):
-            cut = slice(i * lanes, (i + 1) * lanes)
-            x = dot(both, hot_s[at, cut])
-            rd[:, cut] += x[:3 * share] + x[3 * share:]
-        return square + jnp.sum(jnp.sum(r * r, axis=0, keepdims=True), axis=1, keepdims=True)
-
-    square = jnp.zeros((1, 1), F32)
-    for i in range(n_e):
-        q = (me_e + i) % n_e
-        if i:
-            def wait(q=q):
-                copy(r_buf.at[q], r_buf.at[q], ag_ss.at[0], ag_rs.at[q], edge_dev(q)).wait_recv()
-            if own_n == n_e:
-                wait()
-            else:
-                pl.when(q < own_n)(wait)
-        if own_n == n_e:
-            square = use(q, square)
-    if own_n != n_e:
-        square = lax.fori_loop(0, own_n, use, square)
+        square = direct()
 
     rproj = vec[0] * rd[:share]
     for c in (1, 2):
@@ -386,28 +481,6 @@
     loop(n_all - 1, g_arrive)
     for p in range(n_p):
         gin_out[:, p * half:(p + 1) * half] = gf_buf[p].reshape(width, half)
-
-    def sent(i):
-        q = (me_e + i + 1) % n_e
-
-        def go():
-            rs_copy(i, q, me_e).wait_send()
-
-        if own_n == n_e:
-            go()
-        else:
-            pl.when(q < own_n)(go)
-
-    loop(n_e - 1, sent)
-
-    def ag_sent():
-        loop(n_e - 1, lambda i: copy(
-            r_buf.at[me_e], r_buf.at[me_e], ag_ss.at[i], ag_rs.at[me_e], edge_dev((me_e + i + 1) % n_e)).wait_send())
-
-    if own_n == n_e:
-        ag_sent()
-    else:
-        pl.when(me_e < own_n)(ag_sent)
 
     def g_sent(i):
         q = (me_g + i + 1) % g_members
@@ -461,7 +534,8 @@
         name="tiles",
     )(tile_rows, tile_cols, tile_count, tiles, probes)
 
-    own_n = min(n_e, atoms // 128)
+    own_n = atoms // 128 if n_e == 4 else min(n_e, atoms // 128)
+    got_n = max(own_n, n_e)
     piece = atoms // own_n
     g_members = n_e * n_r
     g_own = min(g_members, width // 8)
@@ -493,7 +567,8 @@
             vmem((3 * share, edges), F32),
             vmem((n_e, 1, atoms), F32),
             vmem((own_n, 3 * share, piece), F32),
-            vmem((n_e, 3 * share, piece), F32),
+            vmem((got_n, 3 * share, piece), F32),
+            vmem((own_n, 3 * share, piece), F32),
             vmem((own_n, 3 * share, piece), F32),
             vmem((n_w, 1, atoms + 128), F32),
             vmem((n_p, 1, edges), F32),
@@ -502,8 +577,9 @@
             vmem((n_p, g_own, g_rows, half), F32),
             vmem((g_members, 8, width), F32),
             sem(n_e), sem(n_e),
-            sem(n_e), sem(n_e),
-            sem(n_e), sem(n_e),
+            sem(got_n), sem(got_n),
+            sem(got_n), sem(got_n),
+            sem(got_n), sem(got_n),
             sem(n_w), sem(n_w),
             sem(n_p), sem(n_p),
             sem(g_members), sem(g_members),

time: 79.5 us -> 70.4 us (0.89)
  Pallas kernels: 69.6 us -> 60.2 us
    pallas_call x1, Pallas kernels: 67.6 us -> 57.7 us  [body(): pl.pallas_call(functools.partial(main_kernel, n_e, n_r, n_p, share * n_p)...]
where the time goes in v2:
time: 70.4 us; the launch traced here: 69.7 us
  Pallas kernels  60.2 us (86%)
  local copies, waits for them, and re-layouts  6.8 us (10%)
  between operations  2.71 us (4%)
    pallas_call x1, Pallas kernels, body(): pl.pallas_call(functools.partial(main_kernel, n_e, n_r, n_p, share * n_p)...  57.7 us
    unnamed x25, local copies, waits for them, and re-layouts  6.14 us
    pallas_call x1, Pallas kernels, body(): pl.pallas_call(tile_kernel, out_shape=(jax.ShapeDtypeStruct((3 * share, a...  2.51 us

profile of v2, /device:TPU:0, one launch (start us, length us, event | category | flops | bytes accessed | tf_op | source)
XLA Modules:
  0.0 69.7 jit_solution(13307513262856590904)
XLA Ops:
  0.6 0.0 copy-start.8
  0.6 0.0 copy-start.7
  0.7 0.0 copy-start
  1.4 0.7 reshape.18.w_stiff
  2.1 0.7 %copy.20.vecs = f32[1,3,1536]{2,1,0:T(4,128)S(1)} copy(f32[1,3,1536]{2,0,1:T(1,128)} %param.14) | data formatting | bytes 36864 | tf_op args[1]
  2.8 1.6 %copy.19.probes = s32[3072,64]{1,0:T(8,128)S(1)} copy(s32[3072,64]{0,1:T(8,128)} %param.21) | data formatting | bytes 1572864 | tf_op args[8]
  4.4 0.0 copy-done.8
  4.4 0.0 copy-done.7
  4.4 0.0 copy-done
  4.4 0.0 copy-start.1
  4.4 0.0 copy-start.2
  4.4 0.0 copy-start.3
  4.5 0.0 copy-start.4
  4.5 0.0 copy-start.5
  4.5 0.0 copy-start.6
  4.5 2.5 %tiles.2 = (bf16[192,1024]{1,0:T(8,128)(2,1)S(1)}, f32[192,1024]{1,0:T(8,128)S(1)}) custom-call(s32[1,32]{1,0:T(1,128)S(1)} %copy-done.7, s32[1,32]{1,0:T(1,128)S(1)} %copy-done.8, s32[1,1]{1,0:T(1,128)S(6)} %copy.27.count, bf16[1,32,128,128]{3,2,1,0:T(8,128)(2,1)S(1)} %copy-done, s32[3072,64]{1,0:T(8,128)S(1)} %copy.19.probes), custom_call_target="tpu_custom_call" | custom-call | tf_op jit(solution)/shard_map/tiles/pallas_call | solution.py:520
  7.0 0.0 copy-done.1
  7.0 0.0 copy-done.2
  7.1 57.7 %edges.1 = (f32[3072,64]{1,0:T(8,128)S(1)}, f32[1,128]{1,0:T(1,128)S(1)}, f32[256,256]{1,0:T(8,128)S(1)}, f32[256,128]{1,0:T(8,128)S(1)}, f32[1,256]{1,0:T(1,128)S(1)}, /*index=5*/f32[1,128]{1,0:T(1,128)S(1)}) custom-call(bf16[1,1536,256]{2,1,0:T(8,128)(2,1)S(1)} %copy-done.1, f32[1,3,1536]{2,1,0:T(4,128)S(1)} %copy.20.vecs, s32[1,1536]{1,0:T(1,128)S(1)} %copy-done.4, ...), custom_call_target="tpu_custom_call" | custom-call | tf_op jit(solution)/shard_map/edges/pallas_call | solution.py:548
  64.7 1.3 %copy.21 = f32[1,3072,64]{1,2,0:T(8,128)} copy(f32[1,3072,64]{2,1,0:T(8,128)S(1)} %bitcast.6) | data formatting | bytes 1572864
  66.1 0.7 %copy.29 = f32[256,256]{1,0:T(8,128)} copy(f32[256,256]{1,0:T(8,128)S(1)} %get-tuple-element.36) | data formatting | bytes 524288
  66.8 0.7 copy.30
  67.5 0.6 copy.31
  68.0 0.5 copy.32
  (4 shorter events, 0.0 us)
Async XLA Ops:
  0.6 3.8 %copy-start.8 = (s32[1,32]{1,0:T(1,128)S(1)}, s32[1,32]{1,0:T(1,128)}, u32[]{:S(2)}) copy-start(s32[1,32]{1,0:T(1,128)} %cols.1) | copy-start | bytes 388
  0.6 3.8 %copy-start.7 = (s32[1,32]{1,0:T(1,128)S(1)}, s32[1,32]{1,0:T(1,128)}, u32[]{:S(2)}) copy-start(s32[1,32]{1,0:T(1,128)} %rows.1) | copy-start | bytes 388
  0.7 3.8 %copy-start = (bf16[1,32,128,128]{3,2,1,0:T(8,128)(2,1)S(1)}, bf16[1,32,128,128]{3,2,1,0:T(8,128)(2,1)}, u32[]{:S(2)}) copy-start(bf16[1,32,128,128]{3,2,1,0:T(8,128)(2,1)} %tiles.3) | copy-start | bytes 3145732
  4.4 2.6 %copy-start.1 = (bf16[1,1536,256]{2,1,0:T(8,128)(2,1)S(1)}, bf16[1,1536,256]{2,1,0:T(8,128)(2,1)}, u32[]{:S(2)}) copy-start(bf16[1,1536,256]{2,1,0:T(8,128)(2,1)} %feats.1) | copy-start | bytes 2359300
  4.4 2.6 %copy-start.2 = (bf16[256,256]{1,0:T(8,128)(2,1)S(1)}, bf16[256,256]{1,0:T(8,128)(2,1)}, u32[]{:S(2)}) copy-start(bf16[256,256]{1,0:T(8,128)(2,1)} %w_in.1) | copy-start | bytes 393220
  4.4 2.6 %copy-start.3 = (bf16[256,128]{1,0:T(8,128)(2,1)S(1)}, bf16[256,128]{1,0:T(8,128)(2,1)}, u32[]{:S(2)}) copy-start(bf16[256,128]{1,0:T(8,128)(2,1)} %w_msg.1) | copy-start | bytes 196612
  4.5 2.6 %copy-start.4 = (s32[1,1536]{1,0:T(1,128)S(1)}, s32[1,1536]{1,0:T(1,128)}, u32[]{:S(2)}) copy-start(s32[1,1536]{1,0:T(1,128)} %send.1) | copy-start | bytes 18436
  4.5 2.6 %copy-start.5 = (s32[1,1536]{1,0:T(1,128)S(1)}, s32[1,1536]{1,0:T(1,128)}, u32[]{:S(2)}) copy-start(s32[1,1536]{1,0:T(1,128)} %recv.1) | copy-start | bytes 18436
  4.5 2.6 %copy-start.6 = (f32[128]{0:T(128)S(1)}, f32[128]{0:T(128)}, u32[]{:S(2)}) copy-start(f32[128]{0:T(128)} %param.25) | copy-start | bytes 1540

commit v3 on v2

--- a/solution.py
+++ b/solution.py
@@ -60,8 +60,8 @@
 def tile_kernel(rows, cols, count, tiles, probes, pt_ref, ref_ref, pb, pf, acc):
     n_slots = tiles.shape[1]
     atoms = pt_ref.shape[1]
-    share = probes.shape[1]
-    pv = probes[...].astype(F32)
+    share = probes.shape[0]
+    pv = probes[...].astype(F32).T
     pf[:, :share] = pv
     pb[...] = pv.astype(BF16).reshape(pb.shape)
     acc[...] = jnp.zeros_like(acc)
@@ -88,9 +88,9 @@
     n_e, n_r, n_p, probes_total,
     feats, vecs, send, recv, pt, refs, w_in, w_msg, w_stiff, w_env,
     res_out, mse_out, gin_out, gmsg_out, gstiff_out, genv_out,
-    hot_r, hot_s, pre, latent, proj, contrib, rd,
+    hot_r, hot_s, pre, latent, proj, contrib, rd, res_s, feats_t,
     s_buf, part_buf, got_buf, y_buf, r_buf, w_buf, z_buf, g_buf, gg_buf, gf_buf, v_buf,
-    s_ss, s_rs, rs_ss, rs_rs, y_ss, y_rs, ag_ss, ag_rs, w_ss, w_rs, z_ss, z_rs, g_ss, g_rs, gf_ss, gf_rs, v_ss, v_rs,
+    s_ss, s_rs, rs_ss, rs_rs, y_ss, y_rs, ag_ss, ag_rs, w_ss, w_rs, z_ss, z_rs, g_ss, g_rs, gf_ss, gf_rs, fw_ss, v_ss, v_rs,
 ):
     edges = send.shape[1]
     atoms = pt.shape[1]
@@ -144,7 +144,8 @@
     wenv = w_env[...]
     u = row_dot(wenv, w_msg[...], NT)
     u_hi, u_lo = split(u, 2)
-    readout = stack_rows([w_stiff[...], u_hi, u_lo])
+    ws = w_stiff[...].astype(F32).reshape(1, -1)
+    readout = stack_rows([ws, u_hi, u_lo])
     rows = 256 if edges % 256 == 0 else edges
 
     def forward(i, carry):
@@ -163,9 +164,15 @@
         base = i * 32
         ids = lax.broadcasted_iota(jnp.int32, (32, edges), 0) + base
         at = pl.ds(pl.multiple_of(base, 32), 32)
+        hot_r[at, :] = jnp.where(ids == rcv, 1.0, 0.0).astype(BF16)
+        return carry
+
+    def signed_hots(i, carry):
+        base = i * 32
+        ids = lax.broadcasted_iota(jnp.int32, (32, edges), 0) + base
+        at = pl.ds(pl.multiple_of(base, 32), 32)
         r = jnp.where(ids == rcv, 1.0, 0.0)
         s = jnp.where(ids == snd, 1.0, 0.0)
-        hot_r[at, :] = r.astype(BF16)
         hot_s[at, :] = (s - r).astype(BF16)
         return carry
 
@@ -178,18 +185,18 @@
     edge_dev = lambda e: dev(e, me_r, me_p)
     spread(s_buf, s_ss, s_rs, me_e, n_e, edge_dev)
 
-    vec = [vecs[0, c:c + 1, :] for c in range(3)]
+    vec = [vecs[c] for c in range(3)]
 
     def project(i, carry):
         at = pl.ds(pl.multiple_of(i * lanes, lanes), lanes)
         delta = dot(pt[...], hot_s[:, at])
-        v = vecs[0, :, at]
-        out = v[0:1] * delta[:share]
+        out = vecs[0, :, at] * delta[:share]
         for c in (1, 2):
-            out = out + v[c:c + 1] * delta[c * share:(c + 1) * share]
+            out = out + vecs[c, :, at] * delta[c * share:(c + 1) * share]
         proj[:, at] = out
         return carry
 
+    lax.fori_loop(0, atoms // 32, signed_hots, 0)
     lax.fori_loop(0, edges // lanes, project, 0)
     gathered(s_buf, s_ss, s_rs, me_e, n_e, edge_dev)
     zeta = lw + row_dot(total(s_buf, n_e), hot_r[...])
@@ -197,6 +204,14 @@
     sig_z = sigmoid(zeta)
     for c in range(3):
         contrib[c * share:(c + 1) * share, :] = (stiff * vec[c] * proj[...]).astype(BF16)
+
+    def slope():
+        x = pre[me_p]
+        sg = sigmoid(x)
+        pre[me_p] = sg * (1.0 + x * (1.0 - sg))
+
+    def turn():
+        feats_t[...] = feats[0].T
 
     def tree():
         chunks = r_buf.shape[0]
@@ -238,6 +253,10 @@
                     r_buf[k - 1] = part_buf[k - 1] + y_buf[k - 1]
                     outward(k - 1).start()
 
+            if k == 1:
+                slope()
+            if k == 3:
+                turn()
             if k:
                 @pl.when(is_end)
                 def _(k=k):
@@ -362,6 +381,8 @@
         square = tree()
     else:
         square = direct()
+        slope()
+        turn()
 
     rproj = vec[0] * rd[:share]
     for c in (1, 2):
@@ -381,7 +402,9 @@
     for q in range(own_n):
         for c in range(3):
             x = r_buf[q, c * share:(c + 1) * share, :]
-            res_out[pl.ds(q * piece * 3 + c, piece, stride=3), :] = x.T
+            res_s[pl.ds(q * piece * 3 + c, piece, stride=3), :] = x.T
+    for b in range(3 * atoms // 128):
+        res_out[:, b * 128:(b + 1) * 128] = res_s[b * 128:(b + 1) * 128, :].T
 
     gathered(w_buf, w_ss, w_rs, me_w, n_w, w_dev)
     gathered(z_buf, z_ss, z_rs, me_p, n_p, p_dev)
@@ -399,12 +422,10 @@
     g_members = n_e * n_r
     me_g = me_e * n_r + me_r
     g_dev = lambda f: dev(f // n_r, f % n_r, me_p)
-    v_buf[me_g] = jnp.zeros(v_buf.shape[1:], F32)
     v_buf[me_g, 0:1] = sums[0:1] + sums[1:2]
     v_buf[me_g, 1:2] = sums[2:3] + sums[3:4]
     spread(v_buf, v_ss, v_rs, me_g, g_members, g_dev)
 
-    ws = w_stiff[...].astype(F32)
     ws_half = ws[:, :half]
     u_half = u[:, :half]
     for p in range(1, n_p):
@@ -414,10 +435,8 @@
     dlat = dot(
         stack_rows([dz_hi, dz_lo, wr_hi, wr_hi, wr_lo]),
         stack_rows([ws_half, ws_half, uh_hi, uh_lo, uh_hi]), TN)
-    x = pre[me_p]
-    sg = sigmoid(x)
-    dpre = (dlat * sg * (1.0 + x * (1.0 - sg))).astype(BF16)
-    g_half = dot(feats[0], dpre, TN)
+    dpre = (dlat * pre[me_p]).astype(BF16)
+    g_half = dot(feats_t[...], dpre)
     g_own, g_rows = gf_buf.shape[1], gf_buf.shape[2]
     g_buf[...] = g_half.reshape(g_buf.shape)
 
@@ -434,8 +453,19 @@
 
     loop(g_members - 1, g_send)
 
-    def gf_copy(i, g, p, f):
-        return copy(gf_buf.at[p, g], gf_buf.at[p, g], gf_ss.at[i], gf_rs.at[p, g], all_dev(f))
+    def gf_copy(i, g, f):
+        return copy(gf_buf.at[me_p, g], gf_buf.at[me_p, g], gf_ss.at[i], gf_rs.at[me_p, g], g_dev(f))
+
+    def forward_copy(o, g):
+        return copy(
+            gf_buf.at[me_p, g], gf_buf.at[me_p, g], fw_ss.at[o - 1, g], gf_rs.at[me_p, g],
+            p_dev((me_p + o) % n_p))
+
+    def when_owned(g, fn):
+        if g_own == g_members:
+            fn()
+        else:
+            pl.when(g < g_own)(fn)
 
     def g_own_part():
         gg_buf[me_g] = g_buf[me_g]
@@ -447,10 +477,9 @@
         loop(g_members - 1, wait)
         gf_buf[me_p, me_g] = total(gg_buf, g_members)
 
-        def give(i):
-            gf_copy(i, me_g, me_p, (me_all + i + 1) % n_all).start()
-
-        loop(n_all - 1, give)
+        loop(g_members - 1, lambda i: gf_copy(i, me_g, (me_g + i + 1) % g_members).start())
+        for o in range(1, n_p):
+            forward_copy(o, me_g).start()
 
     if g_own == g_members:
         g_own_part()
@@ -466,19 +495,29 @@
     gmsg_out[...] = dot(stack_rows([q_hi, q_hi, q_lo]), stack_rows([e_hi, e_lo, e_hi]), TN)
     genv_out[...] = row_dot(q_row, w_msg[...])
 
-    def g_arrive(i):
-        f = (me_all + i + 1) % n_all
-        p, g = f % n_p, f // n_p
+    def pass_on(i):
+        g = (me_g + i + 1) % g_members
 
         def go():
-            gf_copy(i, g, p, f).wait_recv()
-
-        if g_own == g_members:
-            go()
-        else:
-            pl.when(g < g_own)(go)
-
-    loop(n_all - 1, g_arrive)
+            gf_copy(i, g, g).wait_recv()
+            for o in range(1, n_p):
+                forward_copy(o, g).start()
+
+        when_owned(g, go)
+
+    loop(g_members - 1, pass_on)
+
+    def from_partner(i):
+        g = (me_g + i) % g_members
+
+        def go():
+            for o in range(1, n_p):
+                p = (me_p + o) % n_p
+                copy(gf_buf.at[p, g], gf_buf.at[p, g], fw_ss.at[o - 1, g], gf_rs.at[p, g], p_dev(p)).wait_recv()
+
+        when_owned(g, go)
+
+    loop(g_members, from_partner)
     for p in range(n_p):
         gin_out[:, p * half:(p + 1) * half] = gf_buf[p].reshape(width, half)
 
@@ -495,13 +534,17 @@
 
     loop(g_members - 1, g_sent)
 
-    def gf_sent():
-        loop(n_all - 1, lambda i: gf_copy(i, me_g, me_p, (me_all + i + 1) % n_all).wait_send())
-
-    if g_own == g_members:
-        gf_sent()
-    else:
-        pl.when(me_g < g_own)(gf_sent)
+    when_owned(me_g, lambda: loop(
+        g_members - 1, lambda i: gf_copy(i, me_g, (me_g + i + 1) % g_members).wait_send()))
+
+    def passed(i):
+        def go():
+            for o in range(1, n_p):
+                forward_copy(o, i).wait_send()
+
+        when_owned(i, go)
+
+    loop(g_members, passed)
 
 
 def body(
@@ -532,7 +575,7 @@
         ],
         compiler_params=pltpu.CompilerParams(vmem_limit_bytes=40 * 2**20),
         name="tiles",
-    )(tile_rows, tile_cols, tile_count, tiles, probes)
+    )(tile_rows, tile_cols, tile_count, tiles, probes.T)
 
     own_n = atoms // 128 if n_e == 4 else min(n_e, atoms // 128)
     got_n = max(own_n, n_e)
@@ -541,14 +584,13 @@
     g_own = min(g_members, width // 8)
     g_rows = width // g_own
     half = width // n_p
-    n_all = n_e * n_r * n_p
     n_w = n_e * n_p
     sem = lambda *shape: pltpu.SemaphoreType.DMA(shape)
     vmem = pltpu.VMEM
     outs = pl.pallas_call(
         functools.partial(main_kernel, n_e, n_r, n_p, share * n_p),
         out_shape=(
-            jax.ShapeDtypeStruct((dim, share), F32),
+            jax.ShapeDtypeStruct((share, dim), F32),
             jax.ShapeDtypeStruct((1, 128), F32),
             jax.ShapeDtypeStruct((width, width), F32),
             jax.ShapeDtypeStruct((width, msg), F32),
@@ -565,6 +607,8 @@
             vmem((share, edges), F32),
             vmem((3 * share, edges), BF16),
             vmem((3 * share, edges), F32),
+            vmem((dim, share), F32),
+            vmem((width, edges), BF16),
             vmem((n_e, 1, atoms), F32),
             vmem((own_n, 3 * share, piece), F32),
             vmem((got_n, 3 * share, piece), F32),
@@ -575,7 +619,7 @@
             vmem((g_own, g_rows, half), F32),
             vmem((g_members, g_rows, half), F32),
             vmem((n_p, g_own, g_rows, half), F32),
-            vmem((g_members, 8, width), F32),
+            vmem((g_members, 2, width), F32),
             sem(n_e), sem(n_e),
             sem(got_n), sem(got_n),
             sem(got_n), sem(got_n),
@@ -583,18 +627,18 @@
             sem(n_w), sem(n_w),
             sem(n_p), sem(n_p),
             sem(g_members), sem(g_members),
-            sem(n_all), sem(n_p, g_members),
+            sem(g_members), sem(n_p, g_members), sem(max(n_p - 1, 1), g_members),
             sem(g_members), sem(g_members),
         ],
         compiler_params=pltpu.CompilerParams(
             collective_id=0, has_side_effects=True, vmem_limit_bytes=48 * 2**20),
         name="edges",
     )(
-        edge_feats, edge_vecs, senders, receivers, pt, refs, w_in, w_msg,
-        w_stiff.reshape(1, -1), w_env.reshape(1, -1),
+        edge_feats, edge_vecs.transpose(1, 0, 2), senders, receivers, pt, refs, w_in, w_msg,
+        w_stiff, w_env.reshape(1, -1),
     )
     residual, mse, g_in, g_msg, g_stiff, g_env = outs
-    return (residual[None], mse[0, :1], g_in, g_msg, g_stiff[0], g_env[0])
+    return (residual.T[None], mse[0, :1], g_in, g_msg, g_stiff[0], g_env[0])
 
 
 def solution(mesh):

time: 70.4 us -> 69.5 us (0.987)
    unnamed x25 -> x29, local copies, waits for them, and re-layouts: 6.14 us -> 6.95 us
where the time goes in v3:
time: 69.5 us
  Pallas kernels  60 us (86%)
  local copies, waits for them, and re-layouts  6.95 us (10%)
  between operations  2.57 us (4%)
    pallas_call x1, Pallas kernels, body(): pl.pallas_call(functools.partial(main_kernel, n_e, n_r, n_p, share * n_p)...  58 us
    unnamed x29, local copies, waits for them, and re-layouts  6.95 us
    pallas_call x1, Pallas kernels, body(): pl.pallas_call(tile_kernel, out_shape=(jax.ShapeDtypeStruct((3 * share, a...  1.97 us

profile of v3, /device:TPU:0, one launch (start us, length us, event | category | flops | bytes accessed | tf_op | source)
XLA Modules:
  0.0 69.5 jit_solution(6260990678122284163)
XLA Ops:
  1.3 0.0 copy-start.10
  1.3 0.0 copy-start.11
  1.3 0.6 copy-done.10
  1.9 0.0 copy-done.11
  2.0 1.2 %copy-done = bf16[1,32,128,128]{3,2,1,0:T(8,128)(2,1)S(1)} copy-done((bf16[1,32,128,128]{3,2,1,0:T(8,128)(2,1)S(1)}, bf16[1,32,128,128]{3,2,1,0:T(8,128)(2,1)}, u32[]{:S(2)}) %copy-start) | copy-done | bytes 1048600
  3.2 1.1 %copy-done.2 = s32[3072,64]{0,1:T(8,128)S(1)} copy-done((s32[3072,64]{0,1:T(8,128)S(1)}, s32[3072,64]{0,1:T(8,128)}, u32[]{:S(2)}) %copy-start.2) | copy-done | bytes 786456
  4.3 0.0 copy-start.6
  4.3 0.0 copy-start.7
  4.3 2.0 %tiles.2 = (bf16[192,1024]{1,0:T(8,128)(2,1)S(1)}, f32[192,1024]{1,0:T(8,128)S(1)}) custom-call(s32[1,32]{1,0:T(1,128)S(1)} %copy-done.10, s32[1,32]{1,0:T(1,128)S(1)} %copy-done.11, s32[1,1]{1,0:T(1,128)S(6)} %copy.25.count, bf16[1,32,128,128]{3,2,1,0:T(8,128)(2,1)S(1)} %copy-done, s32[64,3072]{1,0:T(8,128)S(1)} %bitcast.11), custom_call_target="tpu_custom_call" | custom-call | tf_op jit(solution)/shard_map/tiles/pallas_call | solution.py:563
  6.3 0.0 copy-start.8
  6.3 0.0 copy-start.9
  6.3 0.0 copy-done.1
  6.4 0.0 copy-done.3
  6.4 0.0 copy-done.4
  6.4 0.0 copy-done.5
  6.4 0.0 copy-done.6
  6.4 0.6 copy-done.8
  7.0 0.0 copy-done.9
  7.0 58.0 %edges.1 = (f32[64,3072]{1,0:T(8,128)S(1)}, f32[1,128]{1,0:T(1,128)S(1)}, f32[256,256]{1,0:T(8,128)S(1)}, f32[256,128]{1,0:T(8,128)S(1)}, f32[1,256]{1,0:T(1,128)S(1)}, /*index=5*/f32[1,128]{1,0:T(1,128)S(1)}) custom-call(bf16[1,1536,256]{2,1,0:T(8,128)(2,1)S(1)} %copy-done.1, f32[3,1,1536]{2,1,0:T(1,128)S(1)} %bitcast.12, s32[1,1536]{1,0:T(1,128)S(1)} %copy-done.6, ...), custom_call_target="tpu_custom_call" | custom-call | tf_op jit(solution)/shard_map/edges/pallas_call | solution.py:590
  65.0 0.9 %copy.26 = f32[1,3072,64]{1,2,0:T(8,128)} copy(f32[1,3072,64]{1,2,0:T(8,128)S(1)} %bitcast.10) | data formatting | bytes 1572864
  65.9 0.7 %copy.28 = f32[256,256]{1,0:T(8,128)} copy(f32[256,256]{1,0:T(8,128)S(1)} %get-tuple-element.30) | data formatting | bytes 524288
  66.6 0.7 copy.29
  67.3 0.6 copy.30
  67.8 0.5 copy.31
  (7 shorter events, 0.0 us)
Async XLA Ops:
  1.3 0.7 copy-start.10
  1.3 0.7 copy-start.11
  2.0 1.2 %copy-start = (bf16[1,32,128,128]{3,2,1,0:T(8,128)(2,1)S(1)}, bf16[1,32,128,128]{3,2,1,0:T(8,128)(2,1)}, u32[]{:S(2)}) copy-start(bf16[1,32,128,128]{3,2,1,0:T(8,128)(2,1)} %tiles.3) | copy-start | bytes 3145732
  3.2 1.1 %copy-start.2 = (s32[3072,64]{0,1:T(8,128)S(1)}, s32[3072,64]{0,1:T(8,128)}, u32[]{:S(2)}) copy-start(s32[3072,64]{0,1:T(8,128)} %param.21) | copy-start | bytes 2359300
  4.3 2.0 %copy-start.1 = (bf16[1,1536,256]{2,1,0:T(8,128)(2,1)S(1)}, bf16[1,1536,256]{2,1,0:T(8,128)(2,1)}, u32[]{:S(2)}) copy-start(bf16[1,1536,256]{2,1,0:T(8,128)(2,1)} %feats.1) | copy-start | bytes 2359300
  4.3 2.0 %copy-start.3 = (bf16[256,256]{1,0:T(8,128)(2,1)S(1)}, bf16[256,256]{1,0:T(8,128)(2,1)}, u32[]{:S(2)}) copy-start(bf16[256,256]{1,0:T(8,128)(2,1)} %w_in.1) | copy-start | bytes 393220
  4.3 2.1 %copy-start.4 = (bf16[256,128]{1,0:T(8,128)(2,1)S(1)}, bf16[256,128]{1,0:T(8,128)(2,1)}, u32[]{:S(2)}) copy-start(bf16[256,128]{1,0:T(8,128)(2,1)} %w_msg.1) | copy-start | bytes 196612
  4.3 2.1 %copy-start.5 = (f32[1,3,1536]{2,0,1:T(1,128)S(1)}, f32[1,3,1536]{2,0,1:T(1,128)}, u32[]{:S(2)}) copy-start(f32[1,3,1536]{2,0,1:T(1,128)} %param.14) | copy-start | bytes 55300
  4.3 2.1 %copy-start.6 = (s32[1,1536]{1,0:T(1,128)S(1)}, s32[1,1536]{1,0:T(1,128)}, u32[]{:S(2)}) copy-start(s32[1,1536]{1,0:T(1,128)} %send.1) | copy-start | bytes 18436
  4.3 2.1 %copy-start.7 = (s32[1,1536]{1,0:T(1,128)S(1)}, s32[1,1536]{1,0:T(1,128)}, u32[]{:S(2)}) copy-start(s32[1,1536]{1,0:T(1,128)} %recv.1) | copy-start | bytes 18436
  6.3 0.7 copy-start.8
  6.3 0.7 copy-start.9
